TPU v7x, 32 devices: a whole 2x2x4 slice. The times are simulated.
32 devices in a mesh: dp: 4 (over y, x), fsdp: 8 (over z, core).
Axes of the slice: x: 2, y: 2, z: 4, core: 2. Of those that a mesh axis runs over, the one named last changes fastest.
Arguments:
- tokens: bfloat16 [49152, 768], P(('dp', 'fsdp')), may hold values from -6 to 6
- doc_lengths: int32 [96, 16], P(('dp', 'fsdp')), may hold values from 0 to 512, as said below
- params: bfloat16 [4464640], P(('dp', 'fsdp')), as said below
- cotangent: bfloat16 [49152, 768], P(('dp', 'fsdp')), may hold values from -6 to 6
Outputs:
- output: bfloat16 [49152, 768], P(('dp', 'fsdp'))
- grad_tokens: bfloat16 [49152, 768], P(('dp', 'fsdp'))
- grad_params: float32 [4464640], P(('dp', 'fsdp'))
Inputs may be any that keep to these rules, and one draw needn't show every extreme that they name: Row r holds its documents in order from its first position, doc_lengths[r, j] tokens in slot j (0 for an unused slot); a row's lengths sum to at most 512 and the rest of the row is padding; some row holds one document of 512 tokens. params holds, flattened row-major and in this order: proj_four [4, 768, 384] (query, key, value and convolution-value projections), point_w [768, 384], dense_w [768, 768], ffn_in [2, 384, 1536], ffn_out [2, 1536, 384], depth_w [9, 768], kernel_w [384, 54], query_bias, value_bias, conv_bias, point_bias (each 384), kernel_bias (54), dense_bias, norm1_gain, norm1_shift (each 768), ffn_in_bias (3072), ffn_out_bias, norm2_gain, norm2_shift (each 768); entries after 4460598 are unused.
All inputs are finite; a program needn't handle non-finite values.
Results may differ from a plain program's by a relative error of at most 0.02.
Values may be sent and summed in bfloat16 or wider, within the bound.
A program may use at most 320 MiB of HBM per device.

v0:
```python
import math

import jax
import jax.numpy as jnp
from jax import lax
from jax.experimental import pallas as pl
from jax.experimental.pallas import tpu as pltpu
from jax.sharding import PartitionSpec as P

D = 768
HEADS = 6
HEAD_DIM = 64
ATT = HEADS * HEAD_DIM
FF = 3072
GROUPS = 2
KS = 9
HALF = KS // 2
SLOTS = 16
EPS = 1e-12
LANES = 128
NEG = -1e30
BIG = 3e38
SCALE = HEAD_DIM ** (-0.5)

f32 = jnp.float32
bf16 = jnp.bfloat16
i32 = jnp.int32

FIRST = 5 * D * ATT // LANES
MATRICES = FIRST + (D * D + 2 * D * FF // GROUPS) // LANES
DEPTH_AT = 0
KERNEL_AT = KS * D // LANES
BIAS_AT = KERNEL_AT + ATT * HEADS * KS // LANES
TAIL_AT = BIAS_AT + 4 * ATT // LANES
SMALL = TAIL_AT + 61
KB = HEADS * KS

QB, VB, CB, PB, KBR, DB, N1G, N1S, FIB, FOB, N2G, N2S, DW = range(13)
VROWS = 24
TAIL = [(DB, 6), (N1G, 6), (N1S, 6), (FIB, 24), (FOB, 6), (N2G, 6), (N2S, 6)]

VM = pltpu.VMEM
VMEM_LIMIT = 62 * 1024 * 1024


def nn(a, b):
    return lax.dot_general(a, b, (((1,), (0,)), ((), ())), preferred_element_type=f32)


def nt(a, b):
    return lax.dot_general(a, b, (((1,), (1,)), ((), ())), preferred_element_type=f32)


def tn(a, b):
    return lax.dot_general(a, b, (((0,), (0,)), ((), ())), preferred_element_type=f32)


def iota(shape, axis):
    return lax.broadcasted_iota(i32, shape, axis)


def loop(count, body, unroll=1):
    def step(i, carry):
        body(i)
        return carry

    lax.fori_loop(0, count, step, 0, unroll=unroll)


def tap_perm():
    k, n = iota((LANES, LANES), 0), iota((LANES, LANES), 1)
    head, tap = n & 7, n >> 3
    return jnp.where((k == head * KS + tap) & (head < HEADS) & (tap < KS), 1.0, 0.0).astype(bf16)


def used_taps(shape):
    n = iota(shape, len(shape) - 1)
    return ((n & 7) < HEADS) & ((n >> 3) < KS)


def padded(rows):
    return -(-rows // 16) * 16


class Section:
    def __init__(self, base, kinds, chunk, small, rows, count, inner):
        self.base, self.chunk, self.rows, self.count, self.inner = base, chunk, rows, count, inner
        self.main = sum(n for n, _ in kinds)
        self.small = -(-SMALL // chunk) if small else 0
        self.kinds = kinds + ([(self.small, 1)] if small else [])
        self.used = self.main + self.small
        self.pieces = -(-rows // chunk) + 1
        self.slots = self.pieces + self.small
        self.sources = (chunk - 2) // rows + 2
        self.lead = -(-base // rows)

    def seat(self, v, pick=jnp.where):
        q, r, n = v // 3, v % 3, self.count
        if self.small:
            near = pick(q < n // 4, r * (n // 4) + q, 3 * (n // 4) + v - 3 * (n // 4))
            return pick(v < self.main, near, n - self.small + v - self.main)
        return pick(r < 2, self.lead + 2 * q + r, q)

    def chunk_at(self, d):
        n = self.count
        if self.small:
            quarter = n // 4
            v = jnp.where(d < 3 * quarter, 3 * lax.rem(d, quarter) + d // quarter, d)
            v = jnp.where(v < self.main, v, self.used)
            return jnp.where(d >= n - self.small, self.main + d - (n - self.small), v)
        t = d - self.lead
        v = jnp.where(d < self.main // 3, 3 * d + 2, self.used)
        return jnp.where((t >= 0) & (t < 2 * self.main // 3), 3 * (t // 2) + lax.rem(t, 2), v)

    def start(self, v):
        at = self.base + v * self.chunk
        if self.small:
            at = jnp.where(v >= self.main, MATRICES + (v - self.main) * self.chunk, at)
        return at

    def first_piece(self, i):
        return jnp.maximum(self.rows * i - self.base, 0) // self.chunk

    def of_owner(self, i, k):
        if k < self.pieces:
            v = self.first_piece(i) + k
            ok = v < self.main
        else:
            v = self.main + k - self.pieces + 0 * i
            ok = v >= 0
        at = self.start(v)
        return v, ok & (at < self.rows * (i + 1)) & (at + self.chunk > self.rows * i)

    def of_chunk(self, v, s):
        i = self.start(v) // self.rows + s
        return i, (v < self.used) & (i < self.count) & (self.rows * i < self.start(v) + self.chunk)

    def source_of(self, v, i):
        return i - self.start(v) // self.rows

    def slot_of(self, v, i):
        return jnp.where(v < self.main, v - self.first_piece(i), self.pieces + v - self.main)

    def by_kind(self, v, action):
        at, seen = 0, {}
        for n, per in self.kinds:
            seen.setdefault(per, []).append((at, at + n))
            at += n
        for per, spans in seen.items():
            ok = False
            for lo, hi in spans:
                ok = ((v >= lo) & (v < hi)) | ok
            pl.when(ok)(lambda per=per: action(per))


def sections(count, rows, inner):
    big, little = 24576 // count, 12288 // count
    first = Section(0, [(FIRST // little, 3)], little, True, rows, count, inner)
    kinds = [(D * n // LANES // big, n // LANES) for n in (D, FF // GROUPS)] + [(FF * 3 // big, 3)]
    return first, Section(FIRST, kinds, big, False, rows, count, inner)


class Rows:
    def __init__(self, ref, chunk):
        self.ref, self.chunk = ref, chunk

    def __setitem__(self, where, value):
        v, rows, _ = where
        self.ref[v * self.chunk + rows.start : v * self.chunk + rows.stop, :] = value


def choose(ok, a, b):
    return a if ok else b


def pieces_of(sect, matrices):
    v = 0
    for ref, height, width, col in matrices:
        per = width // LANES
        tall = sect.chunk // per
        for r in range(0, height, tall):
            for c in range(per):
                cols = slice(col + c * LANES, col + (c + 1) * LANES)
                yield sect.seat(v, choose), slice(c * tall, (c + 1) * tall), ref, slice(r, r + tall), cols
            v += 1


def to_frames(sect, part, matrices, small=None):
    for seat, rows, ref, r, c in pieces_of(sect, matrices):
        part[seat, rows, :] = ref[r, c].astype(bf16)
    for k in range(sect.small):
        part[sect.seat(sect.main + k, choose), slice(0, sect.chunk), :] = small[
            k * sect.chunk : (k + 1) * sect.chunk, :
        ].astype(bf16)
    for d in set(range(sect.count)) - {sect.seat(v, choose) for v in range(sect.used)}:
        part[d, slice(0, sect.chunk), :] = jnp.zeros((sect.chunk, LANES), bf16)


def from_frames(sect, buf, matrices, small=None):
    for seat, rows, ref, r, c in pieces_of(sect, matrices):
        ref[r, c] = buf[seat, rows, :]
    for k in range(sect.small):
        small[k * sect.chunk : (k + 1) * sect.chunk, :] = buf[sect.seat(sect.main + k, choose)].astype(f32)


def unpack_small(flat, kw_ref, vec_ref, kwt):
    vec_ref[...] = jnp.zeros_like(vec_ref)
    for row in range(4):
        for c in range(3):
            at = BIAS_AT + row * 3 + c
            vec_ref[row : row + 1, c * LANES : (c + 1) * LANES] = flat[at : at + 1, :]
    for j in range(KS):
        for c in range(6):
            at = DEPTH_AT + j * 6 + c
            vec_ref[DW + j : DW + j + 1, c * LANES : (c + 1) * LANES] = flat[at : at + 1, :]
    at = TAIL_AT
    lane = iota((64, LANES), 1)
    first = pltpu.roll(flat[at : at + 64, :], LANES - KB, 1)
    second = pltpu.roll(flat[at + 1 : at + 65, :], LANES - KB, 1)
    kwt[0:64, :] = jnp.where(lane < LANES - KB, first, second)
    at = 0
    for row, many in TAIL:
        for c in range(many):
            vec_ref[row : row + 1, c * LANES : (c + 1) * LANES] = kwt[at + c : at + c + 1, :]
        at += many
    perm = tap_perm()
    lane8 = iota((16, LANES), 1)
    kb = jnp.broadcast_to(flat[TAIL_AT : TAIL_AT + 1, :], (16, LANES))
    kb = nn(jnp.where(lane8 < KB, kb, 0.0).astype(bf16), perm)
    kb = jnp.where(used_taps((16, LANES)), kb, NEG)
    vec_ref[KBR : KBR + 1, 0:LANES] = kb[0:1]

    lane = iota((8, LANES), 1)
    for a in range(64):
        c0, ln = divmod(a * KB, LANES)
        at = KERNEL_AT + c0
        x = pltpu.roll(flat[pl.ds(at, 8, stride=27), :], (LANES - ln) % LANES, 1)
        if ln + KB > LANES:
            y = pltpu.roll(flat[pl.ds(at + 1, 8, stride=27), :], (LANES - ln) % LANES, 1)
            x = jnp.where(lane < LANES - ln, x, y)
        kwt[pl.ds(a, 8, stride=64), :] = jnp.where(lane < KB, x, 0.0)
    kw_ref[...] = nn(kwt[0:ATT, :].astype(bf16), perm).astype(bf16)


def pack_small(flat, gkw_ref, vec, kwt):
    flat[...] = jnp.zeros_like(flat)
    perm = tap_perm()
    kwt[...] = jnp.zeros_like(kwt)
    kwt[0:ATT, :] = nt(gkw_ref[...].astype(bf16), perm)
    lane = iota((8, LANES), 1)
    for a in range(64):
        c0, ln = divmod(a * KB, LANES)
        at = KERNEL_AT + c0
        x = pltpu.roll(kwt[pl.ds(a, 8, stride=64), :], ln, 1)
        if ln + KB > LANES:
            flat[pl.ds(at, 8, stride=27), :] += jnp.where(lane >= ln, x, 0.0)
            flat[pl.ds(at + 1, 8, stride=27), :] += jnp.where(lane < ln, x, 0.0)
        else:
            flat[pl.ds(at, 8, stride=27), :] += x
    for row in range(4):
        for c in range(3):
            at = BIAS_AT + row * 3 + c
            flat[at : at + 1, :] = vec[row : row + 1, c * LANES : (c + 1) * LANES]
    for j in range(KS):
        for c in range(6):
            at = DEPTH_AT + j * 6 + c
            flat[at : at + 1, :] = vec[DW + j : DW + j + 1, c * LANES : (c + 1) * LANES]
    kwt[...] = jnp.zeros_like(kwt)
    at = 8
    for row, many in TAIL:
        for c in range(many):
            kwt[at + c : at + c + 1, :] = vec[row : row + 1, c * LANES : (c + 1) * LANES]
        at += many
    lane = iota((72, LANES), 1)
    before = pltpu.roll(kwt[7:79, :], KB, 1)
    here = pltpu.roll(kwt[8:80, :], KB, 1)
    at = TAIL_AT
    flat[at : at + 72, :] = jnp.where(lane < KB, before, here)
    kb = jnp.broadcast_to(vec[KBR : KBR + 1, 0:LANES], (16, LANES))
    kb = nt(jnp.where(used_taps((16, LANES)), kb, 0.0).astype(bf16), perm)
    lane = iota((1, LANES), 1)
    flat[at : at + 1, :] = jnp.where(lane < KB, kb[0:1], flat[at : at + 1, :])


class Place:
    def __init__(self, outer, inner):
        self.outer, self.inner, self.count = outer, inner, outer * inner
        self.lines = inner // 2
        dp, fs = lax.axis_index("dp"), lax.axis_index("fsdp")
        self.y, self.x, self.z, self.c = dp // 2, lax.rem(dp, 2), fs // 2, lax.rem(fs, 2)
        self.me = dp * inner + fs

    def coords(self, dy=0, dx=0, z=None, dc=0):
        def flip(v, d):
            return 1 - v if d else v

        z = self.z if z is None else z
        return flip(self.y, dy) * 2 + flip(self.x, dx), z * 2 + flip(self.c, dc)

    def index(self, **d):
        o, i = self.coords(**d)
        return o * self.inner + i

    def device(self, n):
        return n // self.inner, lax.rem(n, self.inner)

    def item(self, t):
        s = (t + 1) // 2
        z = self.z - s if t % 2 else self.z + s
        return z, (z >= 0) & (z < self.lines), s, t % 2 == 1

    def call(self):
        barrier = pltpu.get_barrier_semaphore()
        for n in range(1, self.count):
            peer = self.device(lax.rem(self.me + n, self.count))
            pl.semaphore_signal(barrier, inc=1, device_id=peer, device_id_type=pl.DeviceIdType.MESH)

    def all_here(self):
        pl.semaphore_wait(pltpu.get_barrier_semaphore(), self.count - 1)


class Copies:
    def __init__(self, send, recv):
        self.send, self.recv, self.used, self.made = send, recv, 0, []

    def start(self, src, dst, peer, slot, ok=None, group=None):
        number = self.used if group is None else group
        if group is None:
            self.used += 1
        assert number < self.send.shape[0]

        def make():
            return pltpu.make_async_remote_copy(
                src_ref=src(),
                dst_ref=dst(),
                send_sem=self.send.at[number],
                recv_sem=self.recv.at[slot() if callable(slot) else slot],
                device_id=peer(),
                device_id_type=pl.DeviceIdType.MESH,
            )

        if group is None:
            self.made.append((make, ok))
        guarded(ok, lambda: make().start())

    def sent(self, ref, group):
        pltpu.make_async_copy(ref, ref, self.send.at[group]).wait()

    def arrived(self, dst, slot, ok=None):
        def wait():
            ref = dst()
            pltpu.make_async_copy(ref, ref, self.recv.at[slot]).wait()

        guarded(ok, wait)

    def finish(self):
        for make, ok in self.made:
            guarded(ok, lambda make=make: make().wait_send())


def guarded(ok, action):
    if ok is None:
        action()
    else:
        pl.when(ok())(action)


def half_of(chunk):
    return -(-chunk // 32) * 16


class Gather:
    @staticmethod
    def scratch(sect, inner):
        lines = inner // 2
        items = 2 * lines - 1
        return [
            VM((sect.count, sect.chunk, LANES), bf16),
            VM((sect.slots, sect.chunk, LANES), bf16),
            VM((sect.sources, sect.chunk, LANES), bf16),
            VM((sect.chunk, LANES), f32),
            pltpu.SemaphoreType.DMA((sect.slots + items + 3,)),
            pltpu.SemaphoreType.DMA((sect.sources + 9 * items,)),
        ]

    def __init__(self, sect, place, ownf, lead, scratch):
        self.sect, self.place, self.ownf, self.lead = sect, place, ownf, lead
        self.buf, self.win, self.land, self.frame, send, recv = scratch
        self.copies = Copies(send, recv)
        n = 2 * place.lines - 1
        self.items = n
        self.group = sect.slots + n + 2
        self.Z, self.X, self.Y, self.A, self.B, self.CZ, self.CX, self.CY, self.CD = (sect.sources + n * k for k in range(9))
        cut = half_of(sect.chunk)
        self.half = {"a": pl.ds(0, cut), "b": pl.ds(cut, sect.chunk - cut)}

    def offer(self):
        for k in range(self.sect.slots):
            self.give(k)

    def give(self, k):
        sect, place, me = self.sect, self.place, self.place.me
        v, ok = sect.of_owner(me, k)

        @pl.when(ok)
        def _():
            at = self.lead + sect.start(v) - sect.rows * me
            self.win[k] = self.ownf[pl.ds(at, sect.chunk), :].astype(bf16)

        @pl.when(ok & (sect.seat(v) == me))
        def _():
            self.land[sect.source_of(v, me)] = self.win[k]

        def chunk():
            return sect.of_owner(me, k)[0]

        def away():
            v, ok = sect.of_owner(me, k)
            return ok & (sect.seat(v) != me)

        def source():
            return jnp.clip(sect.source_of(chunk(), me), 0, sect.sources - 1)

        def seat():
            return jnp.clip(sect.seat(chunk()), 0, sect.count - 1)

        self.copies.start(lambda: self.win.at[k], lambda: self.land.at[source()], lambda: place.device(seat()), source, away)

    def form(self):
        sect, me = self.sect, self.place.me
        v = sect.chunk_at(me)
        row = iota((sect.chunk, LANES), 0) + sect.start(v)
        x = None
        for s in range(sect.sources):
            i, ok = sect.of_chunk(v, s)
            self.copies.arrived(lambda: self.land.at[s], s, lambda: ok & (i != me))
            here = self.land[s].astype(f32)
            x = here if x is None else jnp.where(row >= sect.rows * i, here, x)
        self.frame[...] = x

        def settle(per):
            tall = sect.chunk // per
            for c in range(per):
                self.buf[me, c * tall : (c + 1) * tall, :] = self.frame[pl.ds(c, tall, stride=per), :].astype(bf16)

        sect.by_kind(v, settle)

        @pl.when(v >= sect.used)
        def _():
            self.buf[me] = jnp.zeros((sect.chunk, LANES), bf16)

        self.pass_on(0)

    def ref(self, t, which=None, **way):
        def make():
            at = self.place.index(z=self.place.item(t)[0], **way)
            return self.buf.at[at] if which is None else self.buf.at[at, self.half[which]]

        return make

    def ok(self, t):
        return None if t == 0 else lambda: self.place.item(t)[1]

    def same(self, ref, peer, slot, ok, group=True):
        self.copies.start(ref, ref, peer, slot, ok, self.group if group else None)

    def finish(self):
        self.copies.sent(self.buf.at[pl.ds(0, 7 * self.place.lines)], self.group)
        self.copies.finish()

    def beside(self, **way):
        return lambda: self.place.coords(**way)

    def pass_on(self, t):
        place = self.place
        _, _, s, below = place.item(t)
        for way in (1, -1) if t == 0 else ((1,) if below else (-1,)):
            slot = 2 * s + 1 if way > 0 else 2 * s + 2

            def inside(way=way):
                there = place.z + way
                good = (there >= 0) & (there < place.lines)
                return good if t == 0 else good & place.item(t)[1]

            if slot < self.items:
                self.same(self.ref(t), lambda way=way: place.coords(z=place.z + way), self.Z + slot, inside, False)
        ok = self.ok(t)
        self.same(self.ref(t), self.beside(dx=1), self.X + t, ok)
        self.same(self.ref(t), self.beside(dy=1), self.Y + t, ok)
        self.same(self.ref(t), self.beside(dc=1), self.CZ + t, ok)

    def at_distance(self, s):
        return [0] if s == 0 else [2 * s - 1, 2 * s]

    def along(self, s):
        for t in self.at_distance(s):
            self.copies.arrived(self.ref(t), self.Z + t, self.ok(t))
            self.pass_on(t)

    def across(self, s):
        for t in self.at_distance(s):
            ok = self.ok(t)
            self.copies.arrived(self.ref(t, dx=1), self.X + t, ok)
            self.same(self.ref(t, "a", dx=1), self.beside(dy=1), self.A + t, ok)
            self.same(self.ref(t, dx=1), self.beside(dc=1), self.CX + t, ok)
            self.copies.arrived(self.ref(t, dy=1), self.Y + t, ok)
            self.same(self.ref(t, "b", dy=1), self.beside(dx=1), self.B + t, ok)
            self.same(self.ref(t, dy=1), self.beside(dc=1), self.CY + t, ok)

    def diagonal(self):
        for t in range(self.items):
            ok = self.ok(t)
            self.copies.arrived(self.ref(t, "a", dy=1, dx=1), self.A + t, ok)
            self.copies.arrived(self.ref(t, "b", dy=1, dx=1), self.B + t, ok)
            self.same(self.ref(t, dy=1, dx=1), self.beside(dc=1), self.CD + t, ok)

    def rest(self):
        for t in range(self.items):
            for k, way in ((self.CZ, {}), (self.CX, {"dx": 1}), (self.CY, {"dy": 1}), (self.CD, {"dy": 1, "dx": 1})):
                self.copies.arrived(self.ref(t, dc=1, **way), k + t, self.ok(t))


class Scatter:
    @staticmethod
    def scratch(sect, inner):
        lines = inner // 2
        cut = half_of(sect.chunk)
        return [
            VM((4 * lines, sect.chunk, LANES), bf16),
            VM((4 * lines, sect.chunk, LANES), bf16),
            VM((2 * lines, cut, LANES), bf16),
            VM((2 * lines, sect.chunk - cut, LANES), bf16),
            VM((lines, sect.chunk - cut, LANES), bf16),
            VM((lines, cut, LANES), bf16),
            VM((lines, sect.chunk, LANES), bf16),
            VM((sect.chunk, LANES), f32),
            VM((sect.chunk, LANES), f32),
            VM((sect.chunk, LANES), bf16),
            VM((sect.slots, sect.chunk, LANES), bf16),
            pltpu.SemaphoreType.DMA((sect.sources + 6,)),
            pltpu.SemaphoreType.DMA((11 * lines + sect.slots,)),
            pltpu.SemaphoreType.DMA((4 * lines,)),
        ]

    def __init__(self, sect, place, part, out, lead, scratch, close):
        self.close = close
        self.sect, self.place, self.part, self.out, self.lead = sect, place, part, out, lead
        (self.work, self.rc, self.ry, self.rx, self.ry2, self.rx2, self.rz, self.frame, self.flat, self.low, self.land,
         send, recv, self.near) = scratch
        self.copies = Copies(send, recv)
        lines = place.lines
        self.lines = lines
        cut = half_of(sect.chunk)
        self.a, self.b = pl.ds(0, cut), pl.ds(cut, sect.chunk - cut)
        self.C, self.YA, self.XB, self.XA, self.YB, self.Z, self.O = (lines * k for k in (0, 4, 6, 8, 9, 10, 11))
        self.far = list(range(1, lines)) + [0]
        self.group = sect.sources

    def sums(self):
        out = []
        for n in range(self.lines + 2):
            for lag, step in ((0, self.first), (1, self.second), (2, self.third)):
                if 0 <= n - lag < self.lines:
                    out.append(lambda step=step, d=self.far[n - lag]: step(d))
        return out

    def z(self, d):
        return lax.rem(self.place.z + d, self.lines) if d else self.place.z

    def at(self, dy, dx, d):
        return (dy * 2 + dx) * self.lines + d

    def own(self, dy, dx, d):
        k = self.at(dy, dx, d)
        there = self.place.index(dy=dy, dx=dx, z=self.z(d))
        return pltpu.make_async_copy(self.part(there), self.work.at[k], self.near.at[k])

    def core(self, *places):
        place = self.place

        def give(dy, dx, d):
            k = self.at(dy, dx, d)
            self.copies.start(
                lambda: self.part(place.index(dy=dy, dx=dx, z=self.z(d), dc=1)),
                lambda: self.rc.at[k],
                lambda: place.coords(dc=1),
                self.C + k,
                group=self.group,
            )
            if not self.close:
                self.own(dy, dx, d).start()

        for d in places or self.far:
            for dy, dx in ((1, 1), (1, 0), (0, 1), (0, 0)):
                give(dy, dx, d)

    def send(self, k, rows, buf, n, way, slot, group):
        self.copies.start(
            lambda: self.work.at[k, rows],
            lambda: buf.at[n],
            lambda: self.place.coords(**way),
            slot,
            group=self.group + group,
        )

    def finish(self):
        for k, ref in enumerate((self.rc, self.ry, self.rx, self.rx2, self.ry2, self.rz.at[pl.ds(1, self.lines - 1)])):
            self.copies.sent(ref, self.group + k)
        self.copies.finish()

    def got(self, buf, n, slot):
        self.copies.arrived(lambda: buf.at[n], slot)

    def plus(self, k, rows, other):
        self.work[k, rows] = (self.work[k, rows].astype(f32) + other.astype(f32)).astype(bf16)

    def first(self, d):
        lines = self.lines
        for dy, dx in ((1, 1), (1, 0), (0, 1), (0, 0)):
            k = self.at(dy, dx, d)
            if self.close:
                self.got(self.rc, k, self.C + k)
                mine = self.part(self.place.index(dy=dy, dx=dx, z=self.z(d)))[...]
                self.work[k] = (mine.astype(f32) + self.rc[k].astype(f32)).astype(bf16)
            else:
                self.own(dy, dx, d).wait()
                self.got(self.rc, k, self.C + k)
                self.plus(k, pl.ds(0, self.sect.chunk), self.rc[k])
            if dy:
                self.send(k, self.a, self.ry, dx * lines + d, {"dy": 1}, self.YA + dx * lines + d, 1)
            if dx:
                self.send(k, self.b, self.rx, dy * lines + d, {"dx": 1}, self.XB + dy * lines + d, 2)

    def second(self, d):
        n = self.lines + d
        self.got(self.ry, n, self.YA + n)
        self.plus(self.at(0, 1, d), self.a, self.ry[n])
        self.send(self.at(0, 1, d), self.a, self.rx2, d, {"dx": 1}, self.XA + d, 3)
        self.got(self.rx, n, self.XB + n)
        self.plus(self.at(1, 0, d), self.b, self.rx[n])
        self.send(self.at(1, 0, d), self.b, self.ry2, d, {"dy": 1}, self.YB + d, 4)

    def third(self, d):
        k = self.at(0, 0, d)
        self.got(self.ry, d, self.YA + d)
        self.got(self.rx, d, self.XB + d)
        self.got(self.rx2, d, self.XA + d)
        self.got(self.ry2, d, self.YB + d)
        self.plus(k, self.a, self.ry[d].astype(f32) + self.rx2[d].astype(f32))
        self.plus(k, self.b, self.rx[d].astype(f32) + self.ry2[d].astype(f32))
        if d:
            self.copies.start(
                lambda: self.work.at[k],
                lambda: self.rz.at[d],
                lambda: self.place.coords(z=self.z(d)),
                self.Z + d,
                group=self.group + 5,
            )

    def settle(self):
        sect, me = self.sect, self.place.me
        total = self.work[self.at(0, 0, 0)].astype(f32)
        for d in range(1, self.lines):
            self.got(self.rz, d, self.Z + d)
            total = total + self.rz[d].astype(f32)
        self.frame[...] = total

        def spread(per):
            tall = sect.chunk // per
            for c in range(per):
                self.flat[pl.ds(c, tall, stride=per), :] = self.frame[c * tall : (c + 1) * tall, :]

        self.flat[...] = total
        sect.by_kind(sect.chunk_at(me), spread)
        self.low[...] = self.flat[...].astype(bf16)
        for s in range(sect.sources):
            self.give(s)

    def give(self, s):
        sect, me = self.sect, self.place.me
        i, ok = sect.of_chunk(sect.chunk_at(me), s)

        @pl.when(ok & (i == me))
        def _():
            self.land[sect.slot_of(sect.chunk_at(me), i)] = self.low[...]

        def owner():
            return jnp.minimum(sect.of_chunk(sect.chunk_at(me), s)[0], sect.count - 1)

        def slot():
            return jnp.clip(sect.slot_of(sect.chunk_at(me), owner()), 0, sect.slots - 1)

        def away():
            i, ok = sect.of_chunk(sect.chunk_at(me), s)
            return ok & (i != me)

        self.copies.start(
            lambda: self.low, lambda: self.land.at[slot()], lambda: self.place.device(owner()), lambda: self.O + slot(), away
        )

    def take(self):
        sect, me = self.sect, self.place.me
        for k in range(sect.slots):
            v, ok = sect.of_owner(me, k)
            self.copies.arrived(lambda: self.land.at[k], self.O + k, lambda: ok & (sect.seat(v) != me))

            @pl.when(ok)
            def _():
                at = self.lead + sect.start(v) - sect.rows * me
                self.out[pl.ds(at, sect.chunk), :] = self.land[k].astype(f32)


def pumped(due):
    row = pl.program_id(0)

    def pump(point):
        for r, p, step in due:
            if p == point:
                pl.when(row == r)(step)

    return pump


def spread_over(steps, rows, points, spots):
    end = rows * points - 1
    return [(min(n, end) // points, min(n, end) % points, step) for step, n in zip(steps, spots)]


def doc_marks(r, length, len_ref, dcol, tm, mb):
    t = iota((length, LANES), 0)
    u = iota((8, length), 1)
    ends = jnp.int32(0)
    d = jnp.zeros((length, LANES), i32)
    e = jnp.zeros((8, length), i32)
    for j in range(SLOTS):
        ends = ends + len_ref[r, j]
        d = d + (t >= ends).astype(i32)
        e = e + (u >= ends).astype(i32)
    dcol[0:8, :] = jnp.full((8, LANES), -1, i32)
    dcol[8 : 8 + length, :] = d
    dcol[8 + length : 16 + length, :] = jnp.full((8, LANES), -1, i32)
    for j in range(KS):
        at = 8 + j - HALF
        tm[j] = (dcol[at : at + length, :] == d).astype(f32)
    for c in range(length // LANES):
        mb[:, c * LANES : (c + 1) * LANES] = jnp.where(d == e[0:1, c * LANES : (c + 1) * LANES], BIG, NEG)


def tap_lanes(tm, length):
    tap = iota((length, LANES), 1) >> 3
    out = jnp.zeros((length, LANES), f32)
    for j in range(KS):
        out = jnp.where(tap == j, tm[j], out)
    return jnp.where(used_taps((length, LANES)), out, 0.0)


def over_taps(x, op):
    for s in (8, 16, 32, 64):
        x = op(x, pltpu.roll(x, s, 1))
    return x


def fill_emat(emat):
    k, c = iota((2 * LANES, ATT), 0) & (LANES - 1), iota((2 * LANES, ATT), 1)
    for j in range(KS):
        emat[:, j * ATT : (j + 1) * ATT] = jnp.where(k == j * 8 + (c >> 6), 1.0, 0.0).astype(bf16)


def two_parts(x):
    high = x.astype(bf16)
    return jnp.concatenate([high, (x - high.astype(f32)).astype(bf16)], axis=1)


def zero_pads(ref, length):
    for c in range(ref.shape[0]):
        ref[c, 0:8, :] = jnp.zeros((8, LANES), f32)
        ref[c, 8 + length : 16 + length, :] = jnp.zeros((8, LANES), f32)


def fwd_kernel(length, pump, len_ref, tok_ref, wp_ref, pw_ref, kw_ref, vec_ref,
               qkvc_ref, kc_ref, dep_ref, ca_ref, tap_ref, join_ref, lse_ref,
               xs, cs, dcol, tm, mb, emat, acc):
    row = pl.program_id(0)
    pump(0)
    pl.when(row > 0)(lambda: doc_marks(row, length, len_ref, dcol, tm, mb))
    pump(1)
    tok = tok_ref[...]
    zero_pads(xs, length)
    zero_pads(cs, length)
    for c in range(6):
        xs[c, 8 : 8 + length, :] = tok[:, c * LANES : (c + 1) * LANES].astype(f32)
    for m, bias in ((0, QB), (1, None), (2, VB), (3, CB)):
        x = nn(tok, wp_ref[:, m * ATT : (m + 1) * ATT])
        if bias is not None:
            x = x + vec_ref[bias : bias + 1, 0:ATT]
        x = x.astype(bf16)
        qkvc_ref[:, m * ATT : (m + 1) * ATT] = x
        if m == 3:
            for c in range(3):
                cs[c, 8 : 8 + length, :] = x[:, c * LANES : (c + 1) * LANES].astype(f32)

    pump(2)
    step = 64

    for c in range(6):
        w = [vec_ref[DW + j : DW + j + 1, c * LANES : (c + 1) * LANES] for j in range(KS)]
        for r in range(0, length, step):
            total = w[HALF] * xs[c, 8 + r : 8 + r + step, :]
            for j in range(KS):
                if j != HALF:
                    at = 8 + r + j - HALF
                    total = total + w[j] * (xs[c, at : at + step, :] * tm[j, r : r + step, :])
            dep_ref[r : r + step, c * LANES : (c + 1) * LANES] = total.astype(bf16)

    pump(3)
    keyconv = nn(dep_ref[...], pw_ref[...]) + vec_ref[PB : PB + 1, 0:ATT]
    kc_ref[...] = keyconv.astype(bf16)
    ca = (keyconv * qkvc_ref[:, 0:ATT].astype(f32)).astype(bf16)
    ca_ref[...] = ca
    logits = nn(ca, kw_ref[...]) + vec_ref[KBR : KBR + 1, 0:LANES]
    e = jnp.exp(logits - over_taps(logits, jnp.maximum))
    taps = e / over_taps(e, jnp.add)
    tap_ref[...] = taps
    spread = two_parts(taps * tap_lanes(tm, length))
    for j in range(KS):
        if j in (0, 4, 8):
            pump(4 + j // 4)
        if j % 2 == 0:
            t = nn(spread, emat[:, j * ATT : min(j + 2, KS) * ATT])
        for c in range(3):
            at, k = 8 + j - HALF, (j % 2 * 3 + c) * LANES
            part = t[:, k : k + LANES] * cs[c, at : at + length, :]
            if j:
                part = part + acc[:, c * LANES : (c + 1) * LANES]
            if j < KS - 1:
                acc[:, c * LANES : (c + 1) * LANES] = part
            else:
                join_ref[:, ATT + c * LANES : ATT + (c + 1) * LANES] = part.astype(bf16)

    for p in range(3):
        pump(7 + p)
        cols = slice(p * LANES, (p + 1) * LANES)
        q, k, v = (qkvc_ref[:, m * ATT + p * LANES : m * ATT + (p + 1) * LANES] for m in range(3))
        qs = q.astype(f32) * SCALE
        vt = v.astype(f32).T
        lane, sub = iota((length, LANES), 1), iota((LANES, length), 0)
        halves = []
        for h in range(2):
            qh = jnp.where((lane >= HEAD_DIM) == bool(h), qs, 0.0).astype(bf16)
            vh = jnp.where((sub >= HEAD_DIM) == bool(h), vt, 1.0).astype(bf16)
            z = jnp.minimum(nt(k, qh), mb[...])
            top = jnp.max(z, axis=0, keepdims=True)
            o = nn(vh, jnp.exp(z - top).astype(bf16))
            s = o[(1 - h) * HEAD_DIM : (1 - h) * HEAD_DIM + 1, :]
            lse_ref[0, 2 * p + h : 2 * p + h + 1, :] = top + jnp.log(s)
            halves.append(o[h * HEAD_DIM : (h + 1) * HEAD_DIM, :] / s)
        join_ref[:, cols] = jnp.concatenate(halves, axis=0).T.astype(bf16)
    pump(10)


def blocked(rows, cols):
    return pl.BlockSpec((rows, cols), lambda r: (r, 0))


def row_scratch(length):
    return [
        VM((6, length + 16, LANES), f32),
        VM((3, length + 16, LANES), f32),
        VM((length + 16, LANES), i32),
        VM((KS, length, LANES), f32),
        VM((length, length), f32),
        VM((2 * LANES, KS * ATT), bf16),
    ]


FWD_POINTS = 11
FWD_SPOTS = (2, 4, 8, 10, 14, 16, 20, 25, 99)


def run_front(first, second, own, tokens, lengths):
    outer, inner = lax.axis_size("dp"), lax.axis_size("fsdp")
    rows, count = lengths.shape[0], tokens.shape[0]
    length = count // rows
    scratch = row_scratch(length) + [VM((length, ATT), f32)]
    n = len(scratch)
    lead = max(first.chunk, second.chunk)
    more = [
        VM((first.rows + 2 * lead + 16, LANES), f32),
        VM((first.small * first.chunk, LANES), f32),
        VM((512, LANES), f32),
    ]
    m = len(Gather.scratch(first, inner))

    def body(own_ref, len_ref, tok_ref, *refs):
        outs, (dw_ref, fi_ref, fo_ref, wp_ref, pw_ref, kw_ref, vec_ref), refs = refs[:7], refs[7:14], refs[14:]
        rows_refs, (ownf, flat, kwt), refs = refs[:n], refs[n : n + 3], refs[n + 3 :]
        place = Place(outer, inner)
        a = Gather(first, place, ownf, lead, refs[:m])
        b = Gather(second, place, ownf, lead, refs[m:])

        def begin():
            place.call()
            ownf[...] = jnp.zeros_like(ownf)
            ownf[lead : lead + first.rows, :] = own_ref[...].astype(f32)
            _, _, dcol, tm, mb, emat, _ = rows_refs
            fill_emat(emat)
            place.all_here()
            a.offer()
            b.offer()
            doc_marks(0, length, len_ref, dcol, tm, mb)
            a.form()
            for s in range(1, place.lines):
                a.along(s)
                a.across(s - 1)
            a.across(place.lines - 1)
            b.form()
            a.diagonal()
            a.rest()
            from_frames(first, a.buf, [(wp_ref, D, ATT, k * ATT) for k in range(4)] + [(pw_ref, D, ATT, 0)], flat)
            unpack_small(flat, kw_ref, vec_ref, kwt)

        def end():
            a.finish()
            b.rest()
            b.finish()
            from_frames(second, b.buf, ((dw_ref, D, D, 0), (fi_ref, D, FF // GROUPS, 0), (fo_ref, FF, D // GROUPS, 0)))

        steps = []
        for s in range(1, place.lines):
            steps.append(lambda s=s: b.along(s))
            steps.append(lambda s=s: b.across(s - 1))
        steps += [lambda: b.across(place.lines - 1), b.diagonal, end]
        spots = FWD_SPOTS if len(steps) == len(FWD_SPOTS) else [99] * len(steps)
        pump = pumped([(0, 0, begin)] + spread_over(steps, rows, FWD_POINTS, spots))
        fwd_kernel(length, pump, len_ref, tok_ref, wp_ref, pw_ref, kw_ref, vec_ref, *outs, *rows_refs)

    full = pl.BlockSpec(memory_space=VM)
    return pl.pallas_call(
        body,
        grid=(rows,),
        out_shape=[
            jax.ShapeDtypeStruct((count, 4 * ATT), bf16),
            jax.ShapeDtypeStruct((count, ATT), bf16),
            jax.ShapeDtypeStruct((count, D), bf16),
            jax.ShapeDtypeStruct((count, ATT), bf16),
            jax.ShapeDtypeStruct((count, LANES), f32),
            jax.ShapeDtypeStruct((count, D), bf16),
            jax.ShapeDtypeStruct((rows, 8, length), f32),
            jax.ShapeDtypeStruct((D, D), bf16),
            jax.ShapeDtypeStruct((D, FF // GROUPS), bf16),
            jax.ShapeDtypeStruct((FF, D // GROUPS), bf16),
            jax.ShapeDtypeStruct((D, 4 * ATT), bf16),
            jax.ShapeDtypeStruct((D, ATT), bf16),
            jax.ShapeDtypeStruct((ATT, LANES), bf16),
            jax.ShapeDtypeStruct((VROWS, FF), f32),
        ],
        in_specs=[full, pl.BlockSpec(memory_space=pltpu.SMEM), blocked(length, D)],
        out_specs=[
            blocked(length, 4 * ATT),
            blocked(length, ATT),
            blocked(length, D),
            blocked(length, ATT),
            blocked(length, LANES),
            blocked(length, D),
            pl.BlockSpec((1, 8, length), lambda r: (r, 0, 0)),
        ]
        + [full] * 7,
        scratch_shapes=scratch + more + Gather.scratch(first, inner) + Gather.scratch(second, inner),
        compiler_params=pltpu.CompilerParams(vmem_limit_bytes=VMEM_LIMIT, collective_id=0, has_side_effects=True),
        name="front",
    )(own, lengths, tokens)


def mid_kernel(sect, length, len_ref, tok_ref, join_ref, cot_ref, dw_ref, fi_ref, fo_ref, vec_ref,
               out_ref, gf_ref, gj_ref, part_ref, gv_ref,
               gdw_ref, gfi_ref, gfo_ref, xh1, rs1, nl, act, slope, gsec, gsl, wide):
    row = pl.program_id(0)
    fg, dg = FF // GROUPS, D // GROUPS

    @pl.when(row == 0)
    def _():
        for ref in (gdw_ref, gfi_ref, gfo_ref, gv_ref):
            ref[...] = jnp.zeros_like(ref)

    used = jnp.int32(0)
    for j in range(SLOTS):
        used = used + len_ref[row, j]

    def vec(r, n=D):
        return vec_ref[r : r + 1, 0:n]

    step = 128
    halves = [slice(k * (length // 2), (k + 1) * (length // 2)) for k in range(2)]
    for rows in halves:
        gsec[rows, :] = nn(join_ref[rows, :], dw_ref[...])

    def norm1(i):
        at = slice(i * step, (i + 1) * step)
        z = gsec[at, :] + vec(DB) + tok_ref[at, :].astype(f32)
        z = z - jnp.mean(z, axis=1, keepdims=True)
        r = lax.rsqrt(jnp.mean(z * z, axis=1, keepdims=True) + EPS)
        x = z * r
        xh1[at, :] = x
        rs1[at, :] = jnp.broadcast_to(r, (step, LANES))
        nl[at, :] = (x * vec(N1G) + vec(N1S)).astype(bf16)

    for k in range(length // step):
        norm1(k)

    tile = 768
    per = fg // tile

    tiles = [(g, i) for g in range(GROUPS) for i in range(per)]

    def inner(n):
        g, i = tiles[n]
        for rows in halves if n == 0 else [slice(0, length)]:
            wide[n % 2, rows, :] = nn(nl[rows, g * dg : (g + 1) * dg], fi_ref[g * dg : (g + 1) * dg, i * tile : (i + 1) * tile])

    inner(0)
    for n, (g, i) in enumerate(tiles):
        if n + 1 < len(tiles):
            inner(n + 1)
        col = slice(g * fg + i * tile, g * fg + (i + 1) * tile)
        for r in range(0, length, 64):
            x = wide[n % 2, r : r + 64, :] + vec_ref[FIB : FIB + 1, col]
            phi = 0.5 * lax.erf(x * math.sqrt(0.5)) + 0.5
            e = jnp.exp2(x * x * (-0.5 / math.log(2.0)))
            act[r : r + 64, col] = (x * phi).astype(bf16)
            slope[r : r + 64, col] = (phi + x * (1.0 / math.sqrt(2.0 * math.pi)) * e).astype(bf16)

    for rows in halves:
        for g in range(GROUPS):
            gsec[rows, g * dg : (g + 1) * dg] = nn(act[rows, g * fg : (g + 1) * fg], fo_ref[g * fg : (g + 1) * fg, :])

    def rows8(x):
        total = x[0:8]
        for k in range(8, x.shape[0], 8):
            total = total + x[k : k + 8]
        return total

    def norm2(i, carry):
        at = slice(i * step, (i + 1) * step)
        norm = xh1[at, :] * vec(N1G) + vec(N1S)
        z = gsec[at, :] + vec(FOB) + norm
        z = z - jnp.mean(z, axis=1, keepdims=True)
        r = lax.rsqrt(jnp.mean(z * z, axis=1, keepdims=True) + EPS)
        x = z * r
        keep = ((iota((step, 1), 0) + i * step) < used).astype(f32)
        out_ref[at, :] = ((x * vec(N2G) + vec(N2S)) * keep).astype(bf16)
        gf = cot_ref[at, :].astype(f32) * keep
        gx = gf * x
        e = gf * vec(N2G)
        gz = r * (e - jnp.mean(e, axis=1, keepdims=True) - x * jnp.mean(e * x, axis=1, keepdims=True))
        gsec[at, :] = gz
        gsl[at, :] = gz.astype(bf16)
        return (carry[0] + rows8(gx), carry[1] + rows8(gf), carry[2] + rows8(gz))

    none = jnp.zeros((8, D), f32)
    sums = (none, none, none)
    for k in range(length // step):
        sums = norm2(k, sums)

    def add(r, value):
        gv_ref[r : r + 1, 0 : value.shape[1]] += jnp.sum(value, axis=0, keepdims=True)

    for r, value in zip((N2G, N2S, FOB), sums):
        add(r, value)

    def slopes(n):
        g, i = tiles[n]
        at = slice(g * fg + i * tile, g * fg + (i + 1) * tile)
        for rows in halves if n == 0 else [slice(0, length)]:
            wide[n % 2, rows, :] = nt(gsl[rows, g * dg : (g + 1) * dg], fo_ref[at, :])

    slopes(0)
    for n, (g, i) in enumerate(tiles):
        if n + 1 < len(tiles):
            slopes(n + 1)
        at = slice(g * fg + i * tile, g * fg + (i + 1) * tile)
        total = jnp.zeros((8, tile), f32)
        for r in range(0, length, 64):
            x = wide[n % 2, r : r + 64, :] * slope[r : r + 64, at].astype(f32)
            slope[r : r + 64, at] = x.astype(bf16)
            total = total + rows8(x)
        gv_ref[FIB : FIB + 1, at] += jnp.sum(total, axis=0, keepdims=True)
    for rows in halves:
        for g in range(GROUPS):
            gsec[rows, g * dg : (g + 1) * dg] += nt(slope[rows, g * fg : (g + 1) * fg], fi_ref[g * dg : (g + 1) * dg, :])

    def norm1_back(i, carry):
        at = slice(i * step, (i + 1) * step)
        gn = gsec[at, :]
        x = xh1[at, :]
        e = gn * vec(N1G)
        r = rs1[at, :]
        r = jnp.concatenate([r] * (D // LANES), axis=1)
        gz = r * (e - jnp.mean(e, axis=1, keepdims=True) - x * jnp.mean(e * x, axis=1, keepdims=True))
        gf_ref[at, :] = gz.astype(bf16)
        return (carry[0] + rows8(gn * x), carry[1] + rows8(gn), carry[2] + rows8(gz))

    sums = (none, none, none)
    todo = list(enumerate(tiles))
    for k in range(length // step):
        sums = norm1_back(k, sums)
        if k % 2:
            rows = slice((k - 1) * step, (k + 1) * step)
            gj_ref[rows, :] = nt(gf_ref[rows, :], dw_ref[...]).astype(bf16)
        for n, (g, i) in todo[k * len(todo) // (length // step) : (k + 1) * len(todo) // (length // step)]:
            at = slice(g * fg + i * tile, g * fg + (i + 1) * tile)
            gfo_ref[at, :] += tn(act[:, at], gsl[:, g * dg : (g + 1) * dg])
            gfi_ref[g * dg : (g + 1) * dg, i * tile : (i + 1) * tile] += tn(nl[:, g * dg : (g + 1) * dg], slope[:, at])
    for r, value in zip((N1G, N1S, DB), sums):
        add(r, value)
    gdw_ref[...] += tn(join_ref[...], gf_ref[...])

    @pl.when(row == pl.num_programs(0) - 1)
    def _():
        to_frames(sect, part_ref, ((gdw_ref, D, D, 0), (gfi_ref, D, FF // GROUPS, 0), (gfo_ref, FF, D // GROUPS, 0)))


def run_mid(sect, tokens, lengths, joined, cotangent, dw, fi, fo, vec):
    rows, count = lengths.shape[0], tokens.shape[0]
    length = count // rows

    def body(*refs):
        mid_kernel(sect, length, *refs)

    full = pl.BlockSpec(memory_space=VM)
    return pl.pallas_call(
        body,
        grid=(rows,),
        out_shape=[
            jax.ShapeDtypeStruct((count, D), bf16),
            jax.ShapeDtypeStruct((count, D), bf16),
            jax.ShapeDtypeStruct((count, D), bf16),
            jax.ShapeDtypeStruct((sect.count, sect.chunk, LANES), bf16),
            jax.ShapeDtypeStruct((VROWS, FF), f32),
        ],
        in_specs=[pl.BlockSpec(memory_space=pltpu.SMEM)] + [blocked(length, D)] * 3 + [full] * 4,
        out_specs=[blocked(length, D)] * 3 + [full] * 2,
        scratch_shapes=[
            VM((D, D), f32),
            VM((D, FF // GROUPS), f32),
            VM((FF, D // GROUPS), f32),
            VM((length, D), f32),
            VM((length, LANES), f32),
            VM((length, D), bf16),
            VM((length, FF), bf16),
            VM((length, FF), bf16),
            VM((length, D), f32),
            VM((length, D), bf16),
            VM((2, length, 768), f32),
        ],
        compiler_params=pltpu.CompilerParams(vmem_limit_bytes=VMEM_LIMIT),
        name="mid",
    )(lengths, tokens, joined, cotangent, dw, fi, fo, vec)


def bwd_kernel(length, pump, len_ref, tok_ref, qkvc_ref, kc_ref, dep_ref, ca_ref, tap_ref, join_ref, lse_ref, gf_ref, gj_ref,
               wp_ref, pw_ref, kw_ref, vec_ref,
               gt_ref, gp_ref, gpw_ref, gkw_ref, gv_ref,
               ds, cs, dcol, tm, mb, emat, gs, tp, prod, gq, gfour, acc):
    row = pl.program_id(0)

    @pl.when(row == 0)
    def _():
        fill_emat(emat)
        for ref in (gp_ref, gpw_ref, gkw_ref, gv_ref):
            ref[...] = jnp.zeros_like(ref)

    doc_marks(row, length, len_ref, dcol, tm, mb)
    pump(0)
    for ref in (ds, cs, gs, tp):
        zero_pads(ref, length)

    def add(r, value):
        gv_ref[r : r + 1, 0 : value.shape[1]] += jnp.sum(value, axis=0, keepdims=True)

    for p in range(3):
        pump(1 + p)
        cols = slice(p * LANES, (p + 1) * LANES)
        q, k, v = (qkvc_ref[:, m * ATT + p * LANES : m * ATT + (p + 1) * LANES] for m in range(3))
        g = gj_ref[:, cols]
        lane, sub = iota((length, LANES), 1), iota((16, LANES), 1)
        which = iota((16, LANES), 0)
        marks = jnp.where((sub >= HEAD_DIM) == (which >= 8), 1.0, 0.0).astype(bf16)
        dots = g.astype(f32) * join_ref[:, cols].astype(f32)
        high = dots.astype(bf16)
        dots = nt(marks, high) + nt(marks, (dots - high.astype(f32)).astype(bf16))
        qs = q.astype(f32) * SCALE
        kt = k.astype(f32).T.astype(bf16)
        gk, gv, gqt = None, None, []
        for h in range(2):
            own = (lane >= HEAD_DIM) == bool(h)
            qh = jnp.where(own, qs, 0.0).astype(bf16)
            gh = jnp.where(own, g.astype(f32), 0.0).astype(bf16)
            prob = jnp.exp(jnp.minimum(nt(k, qh), mb[...]) - lse_ref[0, 2 * p + h : 2 * p + h + 1, :])
            dsc = (prob * (nt(v, gh) - dots[8 * h : 8 * h + 1, :])).astype(bf16)
            a, b = nn(prob.astype(bf16), gh), nn(dsc, qh)
            gv, gk = (a, b) if h == 0 else (gv + a, gk + b)
            gqt.append(nn(kt, dsc)[h * HEAD_DIM : (h + 1) * HEAD_DIM, :])
        gq[:, cols] = jnp.concatenate(gqt, axis=0).T * SCALE
        gfour[:, ATT + p * LANES : ATT + (p + 1) * LANES] = gk.astype(bf16)
        gfour[:, 2 * ATT + p * LANES : 2 * ATT + (p + 1) * LANES] = gv.astype(bf16)
        gv_ref[VB : VB + 1, cols] += jnp.sum(gv, axis=0, keepdims=True)

    pump(4)
    for c in range(3):
        cs[c, 8 : 8 + length, :] = qkvc_ref[:, 3 * ATT + c * LANES : 3 * ATT + (c + 1) * LANES].astype(f32)
        gs[c, 8 : 8 + length, :] = gj_ref[:, ATT + c * LANES : ATT + (c + 1) * LANES].astype(f32)
    gtaps = None
    for j in range(0, KS, 3):
        for k in range(3):
            for c in range(3):
                at, spot = 8 + j + k - HALF, ((j + k) * 3 + c) * length
                prod[spot : spot + length, :] = (gs[c, 8 : 8 + length, :] * cs[c, at : at + length, :]).astype(bf16)
        blocks = [prod[n * length : (n + 1) * length, :] for n in range(j * 3, j * 3 + 9)]
        x = nt(jnp.concatenate(blocks, axis=1), emat[0:LANES, j * ATT : (j + 3) * ATT])
        gtaps = x if gtaps is None else gtaps + x
    marks = tap_lanes(tm, length)
    gtaps = gtaps * marks
    pump(5)
    taps = jnp.where(used_taps((length, LANES)), tap_ref[...], 0.0)
    glog = taps * (gtaps - over_taps(taps * gtaps, jnp.add))
    add(KBR, glog)
    glog = glog.astype(bf16)
    gkw_ref[...] += tn(ca_ref[...], glog)
    gca = nt(glog, kw_ref[...])

    tp[0, 8 : 8 + length, :] = taps * marks
    tap = iota((length, LANES), 1) >> 3
    moved = jnp.zeros((length, LANES), f32)
    for j in range(KS):
        at = 8 + HALF - j
        moved = jnp.where(tap == j, tp[0, at : at + length, :], moved)
    spread = two_parts(moved)
    for j in range(KS):
        if j % 2 == 0:
            t = nn(spread, emat[:, j * ATT : min(j + 2, KS) * ATT])
        for c in range(3):
            at, k = 8 + HALF - j, (j % 2 * 3 + c) * LANES
            part = t[:, k : k + LANES] * gs[c, at : at + length, :]
            if j:
                part = part + acc[:, c * LANES : (c + 1) * LANES]
            if j < KS - 1:
                acc[:, c * LANES : (c + 1) * LANES] = part
            else:
                gfour[:, 3 * ATT + c * LANES : 3 * ATT + (c + 1) * LANES] = part.astype(bf16)
                gv_ref[CB : CB + 1, c * LANES : (c + 1) * LANES] += jnp.sum(part, axis=0, keepdims=True)

    pump(6)
    gkc = gca * qkvc_ref[:, 0:ATT].astype(f32)
    gquery = gq[...] + gca * kc_ref[...].astype(f32)
    add(QB, gquery)
    gfour[:, 0:ATT] = gquery.astype(bf16)
    add(PB, gkc)
    gkc = gkc.astype(bf16)
    gpw_ref[...] += tn(dep_ref[...], gkc)
    for c in range(3):
        x = nt(gkc, pw_ref[c * 256 : (c + 1) * 256, :])
        ds[2 * c, 8 : 8 + length, :] = x[:, 0:LANES]
        ds[2 * c + 1, 8 : 8 + length, :] = x[:, LANES:]
    pump(7)
    for m in range(2):
        cols = slice(2 * m * ATT, 2 * (m + 1) * ATT)
        gp_ref[:, cols] += tn(tok_ref[...], gfour[:, cols])

    pump(8)
    step = 64
    for c in range(6):
        cols = slice(c * LANES, (c + 1) * LANES)
        w = [vec_ref[DW + j : DW + j + 1, cols] for j in range(KS)]
        sums = [None] * KS
        if c % 2 == 0:
            direct = nt(gfour[...], wp_ref[c * LANES : (c + 2) * LANES, :])
        for r in range(0, length, step):
            tok = tok_ref[r : r + step, cols].astype(f32)
            total = gf_ref[r : r + step, cols].astype(f32) + direct[r : r + step, (c % 2) * LANES : (c % 2 + 1) * LANES]
            for j in range(KS):
                at = 8 + r + j - HALF
                u = ds[c, at : at + step, :]
                if j != HALF:
                    u = u * tm[j, r : r + step, :]
                total = total + w[KS - 1 - j] * u
                u = tok * u
                part = u[0:8]
                for s in range(8, step, 8):
                    part = part + u[s : s + 8]
                sums[j] = part if r == 0 else sums[j] + part
            gt_ref[r : r + step, cols] = total.astype(bf16)
        for j in range(KS):
            gv_ref[DW + KS - 1 - j : DW + KS - j, cols] += jnp.sum(sums[j], axis=0, keepdims=True)
    pump(9)


BWD_POINTS = 10
FIRST_AT, SECOND_AT, THIRD_AT = (2, 3, 6, 10), (5, 9, 13, 15), (9, 13, 16, 17)
SETTLE_AT, TAKE_AT = 21, 26


def run_back(first, second, part, va, tokens, lengths, saved, gf, gj, wp, pw, kw, vec):
    outer, inner = lax.axis_size("dp"), lax.axis_size("fsdp")
    qkvc, kc, dep, ca, taps, joined, lse = saved
    rows, count = lengths.shape[0], tokens.shape[0]
    length = count // rows
    lead = max(first.chunk, second.chunk)
    tall = -(-max(3 * KS * length, first.count * first.chunk) // 16) * 16
    scratch = row_scratch(length) + [
        VM((3, length + 16, LANES), f32),
        VM((1, length + 16, LANES), f32),
        VM((tall, LANES), bf16),
        VM((length, ATT), f32),
        VM((length, 4 * ATT), bf16),
        VM((length, ATT), f32),
    ]
    grads = [VM((D, 4 * ATT), f32), VM((D, ATT), f32), VM((ATT, LANES), f32), VM((VROWS, FF), f32)]
    more = [
        VM((first.rows + 2 * lead + 16, LANES), f32),
        VM((max(first.small * first.chunk, 384), LANES), f32),
        VM((512, LANES), f32),
    ]
    n, m = len(scratch), len(Scatter.scratch(first, inner))

    def body(part_ref, va_ref, *refs):
        ours, (gt_ref, own_ref), refs = refs[:15], refs[15:17], refs[17:]
        rows_refs, sums, refs = refs[:n], refs[n : n + 4], refs[n + 4 :]
        (out, flat, kwt), refs = refs[:3], refs[3:]
        gp_ref, gpw_ref, gkw_ref, gv_ref = sums
        stage = rows_refs[8]
        place = Place(outer, inner)
        a = Scatter(first, place, lambda v: stage.at[pl.ds(v * first.chunk, first.chunk)], out, lead, refs[:m], True)
        b = Scatter(second, place, lambda v: part_ref.at[v], out, lead, refs[m:], False)

        def begin():
            out[...] = jnp.zeros_like(out)
            place.all_here()
            b.core()

        def end():
            gv_ref[...] += va_ref[...]
            pack_small(flat, gkw_ref, gv_ref, kwt)
            to_frames(
                first,
                Rows(stage, first.chunk),
                [(gp_ref, D, ATT, k * ATT) for k in range(4)] + [(gpw_ref, D, ATT, 0)],
                flat,
            )
            steps = a.sums()
            a.core(*a.far[:2])
            for k, step in enumerate(steps):
                if k < len(a.far) - 2:
                    a.core(a.far[2 + k])
                step()
            b.finish()
            a.settle()
            a.take()
            a.finish()
            own_ref[...] = out[lead : lead + first.rows, :]

        due = [(0, 0, begin)]
        for step, spots in ((b.first, FIRST_AT), (b.second, SECOND_AT), (b.third, THIRD_AT)):
            steps = [lambda step=step, d=d: step(d) for d in b.far]
            due += spread_over(steps, rows, BWD_POINTS, list(spots) + [spots[-1]] * (len(steps) - len(spots)))
        due += spread_over([b.settle, b.take], rows, BWD_POINTS, (SETTLE_AT, TAKE_AT))
        pump = pumped(due + [(rows - 1, BWD_POINTS - 1, end)])
        pl.when(pl.program_id(0) == 0)(place.call)
        bwd_kernel(length, pump, *ours, gt_ref, *sums, *rows_refs)

    full = pl.BlockSpec(memory_space=VM)
    return pl.pallas_call(
        body,
        grid=(rows,),
        out_shape=[jax.ShapeDtypeStruct((count, D), bf16), jax.ShapeDtypeStruct((first.rows, LANES), f32)],
        in_specs=[
            pl.BlockSpec(memory_space=pl.ANY),
            full,
            pl.BlockSpec(memory_space=pltpu.SMEM),
            blocked(length, D),
            blocked(length, 4 * ATT),
            blocked(length, ATT),
            blocked(length, D),
            blocked(length, ATT),
            blocked(length, LANES),
            blocked(length, D),
            pl.BlockSpec((1, 8, length), lambda r: (r, 0, 0)),
            blocked(length, D),
            blocked(length, D),
            full,
            full,
            full,
            full,
        ],
        out_specs=[blocked(length, D), full],
        scratch_shapes=scratch + grads + more + Scatter.scratch(first, inner) + Scatter.scratch(second, inner),
        compiler_params=pltpu.CompilerParams(vmem_limit_bytes=VMEM_LIMIT, collective_id=1, has_side_effects=True),
        name="back",
    )(part, va, lengths, tokens, qkvc, kc, dep, ca, taps, joined, lse, gf, gj, wp, pw, kw, vec)


def shards(tokens, doc_lengths, params, cotangent):
    rows = params.shape[0] // LANES
    outer, inner = lax.axis_size("dp"), lax.axis_size("fsdp")
    first, second = sections(outer * inner, rows, inner)
    *saved, dw, fi, fo, wp, pw, kw, vec = run_front(first, second, params.reshape(rows, LANES), tokens, doc_lengths)
    output, gf, gj, part, va = run_mid(second, tokens, doc_lengths, saved[5], cotangent, dw, fi, fo, vec)
    gt, own_grad = run_back(first, second, part, va, tokens, doc_lengths, saved, gf, gj, wp, pw, kw, vec)
    return output, gt, own_grad.reshape(rows * LANES)


def solution(mesh):
    axes = ("dp", "fsdp")
    placed = (P(axes, None), P(axes, None), P(axes), P(axes, None))
    return jax.shard_map(
        shards,
        mesh=mesh,
        in_specs=placed,
        out_specs=(P(axes, None), P(axes, None), P(axes)),
        check_vma=False,
    )
```

profile of v0, /device:TPU:2, one launch (start us, length us, event | category | flops | bytes accessed | tf_op | source)
XLA Modules:
  0.0 236.7 jit_solution(2885353670280561488)
XLA Ops:
  0.6 75.7 %front.1 = (bf16[1536,1536]{1,0:T(8,128)(2,1)}, bf16[1536,384]{1,0:T(8,128)(2,1)}, bf16[1536,768]{1,0:T(8,128)(2,1)}, bf16[1536,384]{1,0:T(8,128)(2,1)}, f32[153...) custom-call(bf16[1090,128]{1,0:T(8,128)(2,1)} %bitcast.3, ...), custom_call_target="tpu_custom_call" | custom-call | tf_op jit(solution)/shard_map/front/pallas_call | solution.py:938
  76.3 51.0 %mid.1 = (bf16[1536,768]{1,0:T(8,128)(2,1)}, bf16[1536,768]{1,0:T(8,128)(2,1)}, bf16[1536,768]{1,0:T(8,128)(2,1)}, bf16[32,768,128]{2,1,0:T(8,128)(2,1)}, f32[24,3072]{1,0:T(8,128)}) custom-call(s32[3,16]{1,0:T(4,128)} %refs_0_.3, bf16[1536,768]{1,0:T(8,128)(2,1)} %refs_1_.3, bf16[1536,768]{1,0:T(8,128)(2,1)} %get-tuple-element.24.refs_2_.refs_7_, ...), custom_call_target="tpu_custom_call" | custom-call | tf_op jit(solution)/shard_map/mid/pallas_call | solution.py:1130
  127.3 105.1 %back.1 = (bf16[1536,768]{1,0:T(8,128)(2,1)}, f32[1090,128]{1,0:T(8,128)}) custom-call(bf16[32,768,128]{2,1,0:T(8,128)(2,1)} %get-tuple-element.30.part_ref, f32[24,3072]{1,0:T(8,128)} %get-tuple-element.31.va_ref, s32[3,16]{1,0:T(4,128)} %refs_0_.3, bf16[1536,768]{1,0:T(8,128)(2,1)} %refs_1_.3, bf16[1536,1536]{1,0:T(8,128)(2,1)} %get-tuple-element.32.refs_2_, ...), custom_call_target="tpu_custom_call" | custom-call | tf_op jit(solution)/shard_map/back/pallas_call | solution.py:1371
  232.3 0.0 copy-start
  232.4 3.3 %copy.9 = bf16[1536,768]{1,0:T(8,128)(2,1)} copy(bf16[1536,768]{1,0:T(8,128)(2,1)} %get-tuple-element.49) | data formatting | bytes 4718592
  235.6 0.0 copy-done
  235.6 0.8 copy.10
Async XLA Ops:
  232.3 3.3 %copy-start = (f32[1090,128]{1,0:T(8,128)S(1)}, f32[1090,128]{1,0:T(8,128)}, u32[]{:S(2)}) copy-start(f32[1090,128]{1,0:T(8,128)} %get-tuple-element.44) | copy-start | bytes 1674244
where the time goes:
time: 241 us; the launch traced here: 237 us
  Pallas kernels  232 us (96%)
  local copies, waits for them, and re-layouts  4.13 us (2%)
    pallas_call x1, Pallas kernels, run_back(): pl.pallas_call(body, grid=(rows,), out_shape=[jax.ShapeDtypeStruct((count...  105 us
    pallas_call x1, Pallas kernels, run_front(): pl.pallas_call(body, grid=(rows,), out_shape=[jax.ShapeDtypeStruct((count...  75.7 us
    pallas_call x1, Pallas kernels, run_mid(): pl.pallas_call(body, grid=(rows,), out_shape=[jax.ShapeDtypeStruct((count...  51 us

commit v1 on v0

--- a/solution.py
+++ b/solution.py
@@ -1398,6 +1398,22 @@
     )(part, va, lengths, tokens, qkvc, kc, dep, ca, taps, joined, lse, gf, gj, wp, pw, kw, vec)
 
 
+def hand_over(x, steps):
+    def body(x_ref, out_ref):
+        out_ref[...] = x_ref[...]
+
+    block = blocked(x.shape[0] // steps, x.shape[1])
+    return pl.pallas_call(
+        body,
+        grid=(steps,),
+        out_shape=jax.ShapeDtypeStruct(x.shape, x.dtype),
+        in_specs=[block],
+        out_specs=block,
+        compiler_params=pltpu.CompilerParams(vmem_limit_bytes=VMEM_LIMIT),
+        name="hand_over",
+    )(x)
+
+
 def shards(tokens, doc_lengths, params, cotangent):
     rows = params.shape[0] // LANES
     outer, inner = lax.axis_size("dp"), lax.axis_size("fsdp")
@@ -1405,7 +1421,7 @@
     *saved, dw, fi, fo, wp, pw, kw, vec = run_front(first, second, params.reshape(rows, LANES), tokens, doc_lengths)
     output, gf, gj, part, va = run_mid(second, tokens, doc_lengths, saved[5], cotangent, dw, fi, fo, vec)
     gt, own_grad = run_back(first, second, part, va, tokens, doc_lengths, saved, gf, gj, wp, pw, kw, vec)
-    return output, gt, own_grad.reshape(rows * LANES)
+    return output, hand_over(gt, 2 * doc_lengths.shape[0]), own_grad.reshape(rows * LANES)
 
 
 def solution(mesh):

time: 241 us -> 242 us (level)
  Pallas kernels: 232 us -> 237 us
  local copies, waits for them, and re-layouts: 4.13 us -> 0.85 us
    pallas_call x0 -> x1, Pallas kernels: none -> 4.96 us  [hand_over(): pl.pallas_call(body, grid=(steps,), out_shape=jax.ShapeDtypeStruct(x.shap...]
    unnamed x4 -> x3, local copies, waits for them, and re-layouts: 4.13 us -> 0.85 us
where the time goes in v1:
time: 242 us; the launch traced here: 238 us
  Pallas kernels  237 us (98%)
    pallas_call x1, Pallas kernels, run_back(): pl.pallas_call(body, grid=(rows,), out_shape=[jax.ShapeDtypeStruct((count...  105 us
    pallas_call x1, Pallas kernels, run_front(): pl.pallas_call(body, grid=(rows,), out_shape=[jax.ShapeDtypeStruct((count...  75.7 us
    pallas_call x1, Pallas kernels, run_mid(): pl.pallas_call(body, grid=(rows,), out_shape=[jax.ShapeDtypeStruct((count...  51 us
    pallas_call x1, Pallas kernels, hand_over(): pl.pallas_call(body, grid=(steps,), out_shape=jax.ShapeDtypeStruct(x.shap...  4.96 us

profile of v1, /device:TPU:2, one launch (start us, length us, event | category | flops | bytes accessed | tf_op | source)
XLA Modules:
  0.0 238.3 jit_solution(1050070130385936388)
XLA Ops:
  0.6 75.7 %front.1 = (bf16[1536,1536]{1,0:T(8,128)(2,1)}, bf16[1536,384]{1,0:T(8,128)(2,1)}, bf16[1536,768]{1,0:T(8,128)(2,1)}, bf16[1536,384]{1,0:T(8,128)(2,1)}, f32[153...) custom-call(bf16[1090,128]{1,0:T(8,128)(2,1)} %bitcast.3, ...), custom_call_target="tpu_custom_call" | custom-call | tf_op jit(solution)/shard_map/front/pallas_call | solution.py:938
  76.3 51.0 %mid.1 = (bf16[1536,768]{1,0:T(8,128)(2,1)}, bf16[1536,768]{1,0:T(8,128)(2,1)}, bf16[1536,768]{1,0:T(8,128)(2,1)}, bf16[32,768,128]{2,1,0:T(8,128)(2,1)}, f32[24,3072]{1,0:T(8,128)}) custom-call(s32[3,16]{1,0:T(4,128)} %refs_0_.3, bf16[1536,768]{1,0:T(8,128)(2,1)} %refs_1_.3, bf16[1536,768]{1,0:T(8,128)(2,1)} %get-tuple-element.24.refs_2_.refs_7_, ...), custom_call_target="tpu_custom_call" | custom-call | tf_op jit(solution)/shard_map/mid/pallas_call | solution.py:1130
  127.3 105.0 %back.1 = (bf16[1536,768]{1,0:T(8,128)(2,1)}, f32[1090,128]{1,0:T(8,128)}) custom-call(bf16[32,768,128]{2,1,0:T(8,128)(2,1)} %get-tuple-element.30.part_ref, f32[24,3072]{1,0:T(8,128)} %get-tuple-element.31.va_ref, s32[3,16]{1,0:T(4,128)} %refs_0_.3, bf16[1536,768]{1,0:T(8,128)(2,1)} %refs_1_.3, bf16[1536,1536]{1,0:T(8,128)(2,1)} %get-tuple-element.32.refs_2_, ...), custom_call_target="tpu_custom_call" | custom-call | tf_op jit(solution)/shard_map/back/pallas_call | solution.py:1371
  232.3 0.0 copy-start
  232.3 5.0 %hand_over.1 = bf16[1536,768]{1,0:T(8,128)(2,1)} custom-call(bf16[1536,768]{1,0:T(8,128)(2,1)} %get-tuple-element.43.x_ref), custom_call_target="tpu_custom_call" | custom-call | tf_op jit(solution)/shard_map/hand_over/pallas_call | solution.py:1406
  237.2 0.0 copy-done
  237.3 0.8 copy.8
Async XLA Ops:
  232.3 5.0 %copy-start = (f32[1090,128]{1,0:T(8,128)S(1)}, f32[1090,128]{1,0:T(8,128)}, u32[]{:S(2)}) copy-start(f32[1090,128]{1,0:T(8,128)} %get-tuple-element.44) | copy-start | bytes 1674244
